TPU v7x, 32 devices: a whole 2x2x4 slice. The times are simulated.
32 devices in a mesh: slab: 8 (over y, x, core), pencil: 4 (over z).
Axes of the slice: x: 2, y: 2, z: 4, core: 2. Of those that a mesh axis runs over, the one named last changes fastest.
Arguments:
- adjoint_vort: float32 [3, 16, 512, 512], P(None, 'slab', 'pencil'), may hold values from -6 to 6
- omega_ckpt: float32 [2, 3, 16, 512, 512], P(None, None, 'slab', 'pencil'), may hold values from -6 to 6
- cell_shift: int32 [2, 16, 512, 512], P(None, 'slab', 'pencil'), may hold values from -2 to 2
- move_count: int32 [2, 8, 4, 2], P(None, 'slab', 'pencil'), may hold values from 32 to 256, as said below
- move_blocks: int32 [2, 8, 4, 2, 256], P(None, 'slab', 'pencil'), may hold values from 0 to 511, as said below
Outputs:
- adjoint_out: float32 [3, 16, 512, 512], P(None, 'slab', 'pencil')
Inputs may be any that keep to these rules, and one draw needn't show every extreme that they name: `move_count`: in every substep and direction some device has 256 live entries and some device 256 // 8. `move_blocks`: for each substep and device, the 512 entries are the plane-block numbers 0 to 511, each once.
All inputs are finite; a program needn't handle non-finite values.
Results may differ from a plain program's by a relative error of at most 0.00025.
Values sent between devices are 32-bit elements; how exact they have to be, the bound alone decides.
A program may use at most 64 MiB of HBM per device.

v0:
```python
import functools

import jax
import jax.numpy as jnp
import ml_dtypes
import numpy as np
from jax import lax
from jax.experimental import pallas as pl
from jax.experimental.pallas import tpu as pltpu
from jax.sharding import PartitionSpec as P

BL = 128
TILE = 16
AWAY = 16
MESH = pl.DeviceIdType.MESH
bf16 = jnp.bfloat16
f32 = jnp.float32

time_step = 0.25


def tables(rows, groups, depth):
    k = np.arange(depth)
    phase = 2.0 * np.pi * ((k[:, None] * k[None, :]) % depth) / depth
    cas = np.cos(phase) + np.sin(phase)
    slope = np.sin(2.0 * np.pi * k / depth)[:, None] * (np.cos(phase) - np.sin(phase))
    ev_z = 4.0 * np.sin(np.pi * k / depth) ** 2
    j = np.arange(1, rows + 1)
    norm = np.sqrt(2.0 / (rows + 1))
    sine = norm * np.sin(np.pi * j[:, None] * j[None, :] / (rows + 1))
    ghost = np.zeros((rows + 2, rows))
    ghost[1:-1] = sine
    dsine = 0.5 * (ghost[2:] - ghost[:-2])
    ev_y = 4.0 * np.sin(np.pi * j / (2.0 * (rows + 1))) ** 2
    inverse = 1.0 / (ev_y[:, None] + ev_z[None, :])
    decay = np.exp(-2.0 * np.arcsinh(np.sqrt(ev_z[1:]) / 2.0))[None, :]
    y = np.arange(-1, rows + 1)[:, None]
    left = np.zeros((rows + 2, depth))
    left[:, 0] = (rows - y[:, 0]) / (rows + 1.0)
    left[:, 1:] = decay ** (y + 1.0) * (1.0 - decay ** (2.0 * (rows - y))) / (1.0 - decay ** (2.0 * (rows + 1)))
    right = left[::-1]
    quad = np.zeros((rows + 2, depth))
    quad[:, 0] = (y[:, 0] + 1) * (rows - y[:, 0]) / 2.0
    bend = np.stack([left[1:-1], right[1:-1], quad[1:-1]])
    dbend = np.stack([0.5 * (t[2:] - t[:-2]) for t in (left, right, quad)])
    near, far = left[1], left[rows]
    size = 2 * groups
    system = np.tile(np.eye(size), (depth, 1, 1))
    for p in range(groups):
        before, after = 2 * ((p - 1) % groups) + 1, 2 * ((p + 1) % groups)
        system[:, 2 * p, before] -= near
        system[:, 2 * p, after] -= far
        system[:, 2 * p + 1, before] -= far
        system[:, 2 * p + 1, after] -= near
    solve = np.zeros_like(system)
    solve[1:] = np.linalg.inv(system[1:])
    solve[0] = np.linalg.pinv(system[0], rcond=1e-9)
    coef = np.zeros((3, groups, 3, depth))
    for out, row in ((0, 2 * (groups - 1) + 1), (1, 2 * (1 % groups))):
        for q in range(groups):
            coef[out, q, 0] = solve[:, row, 2 * q]
            coef[out, q, 1] = solve[:, row, 2 * q + 1]
            both = solve[0, row, 2 * q] + solve[0, row, 2 * q + 1]
            every = solve[0, row].sum() / groups
            coef[out, q, 2, 0] = (both - every) * rows / 2.0
    coef[2, :, 2, 0] = -1.0 / groups
    coef[2, 0, 2, 0] += 1.0
    return cas, slope, sine, dsine, inverse, bend, dbend, coef


def shifted_deposit(values, shifts):
    total = jnp.zeros(values.shape, jnp.float32)
    for amount in (-2, -1, 0, 1, 2):
        picked = jnp.where(shifts == amount, values, 0.0)
        total = total + jnp.roll(picked, amount, axis=-1)
    return total


def split_table(table):
    table = np.asarray(table, np.float32)
    high = table.astype(ml_dtypes.bfloat16)
    low = (table - high.astype(np.float32)).astype(ml_dtypes.bfloat16)
    return high, low


def stacked_table(table):
    high, low = split_table(table)
    top = np.concatenate([high, high], 1)
    return np.concatenate([top, np.concatenate([low, np.zeros_like(low)], 1)], 0)


def split(value):
    high = value.astype(bf16)
    return high, (value - high.astype(f32)).astype(bf16)


def dot(left, right):
    return jnp.dot(left, right, preferred_element_type=f32)


def kernel(
    sizes,
    lists,
    adjoint_in,
    shifts_in,
    ends,
    omega_hbm,
    *refs,
):
    steps, planes, rows, depth, groups, slabs, capacity, count = sizes
    table_hbm = refs[:count]
    out = refs[count]
    table_vmem = refs[count + 1 : 2 * count + 1]
    (
        omega_in,
        code,
        lam,
        current,
        vortex,
        lam_send,
        lam_recv,
        omega_send,
        omega_recv,
        field,
        field_recv,
        edges,
        source_hi,
        source_lo,
        modes,
        spec_hi,
        spec_lo,
        load_sem,
        omega_sem,
        lam_ssem,
        lam_rsem,
        omega_ssem,
        omega_rsem,
        field_ssem,
        field_rsem,
        edge_ssem,
        edge_rsem,
    ) = refs[2 * count + 1 :]
    cas_hi, cas_lo, slope_hi, slope_lo, sine, dsine, inverse, bend, dbend, coef = table_vmem
    slab = lax.axis_index("slab")
    pencil = lax.axis_index("pencil")
    onward = lax.rem(slab + 1, slabs)
    back = lax.rem(slab + slabs - 1, slabs)
    others = [lax.rem(pencil + groups - d, groups) for d in range(1, groups)]

    omega_load = pltpu.make_async_copy(omega_hbm, omega_in, omega_sem.at[0])
    omega_load.start()
    loads = [
        pltpu.make_async_copy(table_hbm[t], table_vmem[t], load_sem.at[t]) for t in range(count)
    ]
    for load in loads:
        load.start()

    barrier = pltpu.get_barrier_semaphore()
    for target in (onward, back):
        pl.semaphore_signal(barrier, inc=1, device_id={"slab": target}, device_id_type=MESH)
    for target in others:
        pl.semaphore_signal(barrier, inc=1, device_id={"pencil": target}, device_id_type=MESH)

    sent = []

    def send(source, target, ssem, rsem, to):
        copy = pltpu.make_async_remote_copy(
            src_ref=source,
            dst_ref=target,
            send_sem=ssem,
            recv_sem=rsem,
            device_id=to,
            device_id_type=MESH,
        )
        copy.start()
        sent.append(copy)
        return copy

    def make_code(s):
        row_id = lax.broadcasted_iota(jnp.int32, (rows, capacity), 0)
        block_id = lax.broadcasted_iota(jnp.int32, (depth, capacity), 0) >> (BL.bit_length() - 1)
        for direction, x in ((0, planes - 1), (1, 0)):
            at = (s * 2 + direction) * 2
            row_hit = jnp.where(row_id == lists[at : at + 1, :], 1.0, 0.0).astype(bf16)
            block_hit = jnp.where(block_id == lists[at + 1 : at + 2, :], 1.0, 0.0).astype(bf16)
            hit = lax.dot_general(
                row_hit, block_hit, (((1,), (1,)), ((), ())), preferred_element_type=f32
            )
            code[s, x] = shifts_in[s, x] + jnp.where(hit > 0.5, AWAY, 0)

    def deposit(s, values, stay, leave):
        def tile(i, carry):
            at = pl.ds(pl.multiple_of(i * 8, 8), 8)
            for x in range(planes):
                direction = 0 if x == planes - 1 else 1
                mine = code[s, x, at, :]
                carried = [values[c, x, at, :] for c in range(3)]
                kept = [jnp.where(mine == 0, v, 0.0) for v in carried]
                gone = [jnp.where(mine == AWAY, v, 0.0) for v in carried]
                for amount in (-2, -1, 1, 2):
                    turned = pltpu.roll(mine, amount % depth, 1)
                    here = turned == amount
                    there = turned == amount + AWAY
                    for c in range(3):
                        moved = pltpu.roll(carried[c], amount % depth, 1)
                        kept[c] = kept[c] + jnp.where(here, moved, 0.0)
                        gone[c] = gone[c] + jnp.where(there, moved, 0.0)
                for c in range(3):
                    stay[c, x, at, :] = kept[c]
                    leave[direction, c, at, :] = gone[c]
            return carry

        lax.fori_loop(0, rows // 8, tile, 0)

    def send_lam(s):
        copies = []
        for c in range(3):
            copies.append(
                [
                    send(
                        lam_send.at[s, d, c],
                        lam_recv.at[s, d, c],
                        lam_ssem.at[s, d, c],
                        lam_rsem.at[s, d, c],
                        {"slab": (onward, back)[d]},
                    )
                    for d in range(2)
                ]
            )
        return copies

    def send_omega(s):
        return [
            send(
                omega_send.at[s, d],
                omega_recv.at[s, d],
                omega_ssem.at[s, d],
                omega_rsem.at[s, d],
                {"slab": (onward, back)[d]},
            )
            for d in range(2)
        ]

    make_code(0)
    deposit(0, adjoint_in, lam, lam_send.at[0])
    pl.semaphore_wait(barrier, 2 + groups - 1)
    lam_copies = send_lam(0)
    omega_load.wait()
    deposit(0, omega_in.at[0], vortex.at[0], omega_send.at[0])
    omega_copies = send_omega(0)
    for load in loads:
        load.wait()

    first = (lax.broadcasted_iota(jnp.int32, (1, depth), 1) == 0).astype(f32)
    for s in range(steps):
        edges[s, 0] = jnp.zeros((3, 8, depth), f32)
        for c in range(3):
            for copy in lam_copies[c]:
                copy.wait_recv()

            def gather(i, carry):
                at = pl.ds(pl.multiple_of(i * TILE, TILE), TILE)
                for x in range(planes):
                    total = lam[c, x, at, :]
                    if x == 0:
                        total = total + lam_recv[s, 0, c, at, :]
                    if x == planes - 1:
                        total = total + lam_recv[s, 1, c, at, :]
                    lam[c, x, at, :] = total
                    high, low = split(total)
                    to = pl.ds(pl.multiple_of(x * rows + i * TILE, TILE), TILE)
                    source_hi[to, :] = high
                    source_lo[to, :] = low
                return carry

            lax.fori_loop(0, rows // TILE, gather, 0)
            hat = (
                dot(source_hi[...], cas_hi[...])
                + dot(source_lo[...], cas_hi[...])
                + dot(source_hi[...], cas_lo[...])
            )
            for x in range(planes):
                part = hat[x * rows : (x + 1) * rows]
                mean = jnp.sum(part, axis=0, keepdims=True) * (first / rows)
                high, low = split(part - mean)
                wide = dot(sine[...], jnp.concatenate([high, low], 0))
                amount = (wide[:rows] + wide[rows:]) * inverse[...]
                n = c * planes + x
                for e in range(2):
                    edges[s, 0, e, n : n + 1, :] = jnp.sum(
                        amount * ends[:, e : e + 1], axis=0, keepdims=True
                    )
                edges[s, 0, 2, n : n + 1, :] = mean
                high, low = split(amount)
                modes[n, :rows, :] = high
                modes[n, rows:, :] = low
        edge_copies = [
            send(
                edges.at[s, 0],
                edges.at[s, d],
                edge_ssem.at[s, d - 1],
                edge_rsem.at[s, d - 1],
                {"pencil": others[d - 1]},
            )
            for d in range(1, groups)
        ]
        for copy in edge_copies:
            copy.wait_recv()
        ghosts = []
        for o in range(3):
            total = jnp.zeros((8, depth), f32)
            for q in range(groups):
                for e in range(3):
                    total = total + coef[o, q, e : e + 1, :] * edges[s, q, e]
            ghosts.append(total)
        for slot, c, matrix, shape in (
            (0, 2, dsine, dbend),
            (1, 0, dsine, dbend),
            (2, 1, sine, bend),
            (3, 0, sine, bend),
        ):
            for x in range(planes):
                n = c * planes + x
                wide = dot(matrix[...], modes[n])
                value = wide[:rows] + wide[rows:]
                for o in range(3):
                    value = value + shape[o] * ghosts[o][n : n + 1]
                high, low = split(value)
                spec_hi[slot, x * rows : (x + 1) * rows, :] = high
                spec_lo[slot, x * rows : (x + 1) * rows, :] = low

        def along_z(slot, hi, lo):
            return (
                dot(spec_hi[slot], hi[...])
                + dot(spec_lo[slot], hi[...])
                + dot(spec_hi[slot], lo[...])
            )

        field_copies = []
        scale = 1.0 / depth
        for c in (1, 2, 0):
            if c == 1:
                got = along_z(3, slope_hi, slope_lo) * scale
            elif c == 2:
                got = along_z(1, cas_hi, cas_lo) * -scale
            else:
                got = (along_z(0, cas_hi, cas_lo) - along_z(2, slope_hi, slope_lo)) * scale
            for x in range(planes):
                field[s, c, x] = got[x * rows : (x + 1) * rows]
            for d, x in ((0, planes - 1), (1, 0)):
                field_copies.append(
                    send(
                        field.at[s, c, x],
                        field_recv.at[s, d, c],
                        field_ssem.at[s, d, c],
                        field_rsem.at[s, d, c],
                        {"slab": (onward, back)[d]},
                    )
                )
        arriving = omega_copies
        if s + 1 < steps:
            make_code(s + 1)
            deposit(s + 1, omega_in.at[s + 1], vortex.at[s + 1], omega_send.at[s + 1])
            omega_copies = send_omega(s + 1)
        for copy in arriving:
            copy.wait_recv()
        for copy in field_copies:
            copy.wait_recv()
        result = current if s + 1 < steps else out

        def update(i, carry):
            at = pl.ds(pl.multiple_of(i * 8, 8), 8)
            for x in range(planes):
                w = [vortex[s, c, x, at, :] for c in range(3)]
                if x == 0:
                    w = [w[c] + omega_recv[s, 0, c, at, :] for c in range(3)]
                if x == planes - 1:
                    w = [w[c] + omega_recv[s, 1, c, at, :] for c in range(3)]
                g = [field[s, c, x, at, :] for c in range(3)]
                crossed = (
                    w[1] * g[2] - w[2] * g[1],
                    w[2] * g[0] - w[0] * g[2],
                    w[0] * g[1] - w[1] * g[0],
                )
                for c in range(3):
                    if x == 0:
                        low = field_recv[s, 0, c, at, :]
                    else:
                        low = field[s, c, x - 1, at, :]
                    if x == planes - 1:
                        high = field_recv[s, 1, c, at, :]
                    else:
                        high = field[s, c, x + 1, at, :]
                    slope_x = (high - low) * 0.5
                    result[c, x, at, :] = lam[c, x, at, :] + time_step * (
                        crossed[c] + w[0] * slope_x
                    )
            return carry

        lax.fori_loop(0, rows // 8, update, 0)
        if s + 1 < steps:
            deposit(s + 1, current, lam, lam_send.at[s + 1])
            lam_copies = send_lam(s + 1)
    for copy in sent:
        copy.wait_send()


def shards(adjoint_vort, omega_ckpt, cell_shift, move_count, move_blocks):
    _, planes, rows, depth = adjoint_vort.shape
    steps = omega_ckpt.shape[0]
    groups, slabs = lax.axis_size("pencil"), lax.axis_size("slab")
    capacity = move_blocks.shape[-1]
    assert planes == 2
    per_row = depth // BL
    chosen = move_blocks[:, 0, 0]
    alive = jnp.arange(capacity, dtype=jnp.int32) < move_count[:, 0, 0][..., None]
    lists = jnp.stack([jnp.where(alive, chosen // per_row, -1), chosen % per_row], 2)
    lists = lists.reshape(steps * 4, capacity)

    cas, slope, sine, dsine, inverse, bend, dbend, coef = tables(rows, groups, depth)
    ends = np.zeros((rows, 128), np.float32)
    ends[:, 0], ends[:, 1] = sine[0], sine[-1]
    held = [
        *split_table(cas),
        *split_table(slope),
        stacked_table(sine),
        stacked_table(dsine),
        np.asarray(inverse, np.float32),
        np.asarray(bend, np.float32),
        np.asarray(dbend, np.float32),
        np.asarray(coef, np.float32),
    ]
    held = [jnp.asarray(t) for t in held]
    count = len(held)
    dma = pltpu.SemaphoreType.DMA
    vm = pltpu.VMEM
    scratch = [vm(t.shape, t.dtype) for t in held] + [
        vm(omega_ckpt.shape, f32),
        vm((steps, planes, rows, depth), jnp.int32),
        vm((3, planes, rows, depth), f32),
        vm((3, planes, rows, depth), f32),
        vm((steps, 3, planes, rows, depth), f32),
        vm((steps, 2, 3, rows, depth), f32),
        vm((steps, 2, 3, rows, depth), f32),
        vm((steps, 2, 3, rows, depth), f32),
        vm((steps, 2, 3, rows, depth), f32),
        vm((steps, 3, planes, rows, depth), f32),
        vm((steps, 2, 3, rows, depth), f32),
        vm((steps, groups, 3, 8, depth), f32),
        vm((planes * rows, depth), bf16),
        vm((planes * rows, depth), bf16),
        vm((3 * planes, 2 * rows, depth), bf16),
        vm((4, planes * rows, depth), bf16),
        vm((4, planes * rows, depth), bf16),
        dma((count,)),
        dma((1,)),
        dma((steps, 2, 3)),
        dma((steps, 2, 3)),
        dma((steps, 2)),
        dma((steps, 2)),
        dma((steps, 2, 3)),
        dma((steps, 2, 3)),
        dma((steps, groups - 1)),
        dma((steps, groups - 1)),
    ]
    sizes = (steps, planes, rows, depth, groups, slabs, capacity, count)
    local = pl.BlockSpec(memory_space=pltpu.VMEM)
    return pl.pallas_call(
        functools.partial(kernel, sizes),
        out_shape=jax.ShapeDtypeStruct(adjoint_vort.shape, f32),
        in_specs=[local] * 4 + [pl.BlockSpec(memory_space=pl.ANY)] * (1 + count),
        out_specs=local,
        scratch_shapes=scratch,
        compiler_params=pltpu.CompilerParams(
            collective_id=0, has_side_effects=True, vmem_limit_bytes=56 * 1024 * 1024
        ),
    )(lists, adjoint_vort, cell_shift, jnp.asarray(ends), omega_ckpt, *held)


def solution(mesh):
    return jax.shard_map(
        shards,
        mesh=mesh,
        in_specs=(
            P(None, "slab", "pencil", None),
            P(None, None, "slab", "pencil", None),
            P(None, "slab", "pencil", None),
            P(None, "slab", "pencil", None),
            P(None, "slab", "pencil", None, None),
        ),
        out_specs=P(None, "slab", "pencil", None),
        check_vma=False,
    )
```

profile of v0, /device:TPU:0, one launch (start us, length us, event | category | flops | bytes accessed | tf_op | source)
XLA Modules:
  0.0 128.4 jit_solution(7895585331948605290)
XLA Ops:
  0.0 0.8 compare_select_fusion
  0.8 0.6 reshape.115.lists
  1.4 124.2 %shard_map.154 = f32[3,2,128,512]{3,2,1,0:T(8,128)} custom-call(s32[8,256]{1,0:T(8,128)} %reshape.115.lists, f32[3,2,128,512]{3,2,1,0:T(8,128)} %adjoint_in.1, s32[2,2,128,512]{3,2,1,0:T(8,128)} %shifts_in.1, f32[128,128]{1,0:T(8,128)} %constant.61.clone.ends, f32[2,3,2,128,512]{4,3,2,1,0:T(8,128)} %omega_hbm.1, bf16[512,512]{1,0:T(8,128)(2,1)} %constant.51.clone.refs_0_, ...), custom_call_target="tpu_custom_call" | custom-call | tf_op jit(solution)/shard_map/pallas_call | solution.py:468
  125.6 2.8 %copy.19 = f32[3,2,128,512]{3,2,1,0:T(8,128)} copy(f32[3,2,128,512]{3,2,1,0:T(8,128)} %shard_map.154) | data formatting | bytes 3145728
  (2 shorter events, 0.0 us)
where the time goes:
time: 129 us; the launch traced here: 128 us
  Pallas kernels  124 us (96%)
  local copies, waits for them, and re-layouts  3.38 us (3%)
    pallas_call x1, Pallas kernels, shards(): pl.pallas_call(functools.partial(kernel, sizes), out_shape=jax.ShapeDtype...  124 us
    unnamed x1, local copies, waits for them, and re-layouts  2.76 us

commit v1 on v0

--- a/solution.py
+++ b/solution.py
@@ -101,6 +101,7 @@
 def kernel(
     sizes,
     lists,
+    lists_t,
     adjoint_in,
     shifts_in,
     ends,
@@ -139,6 +140,17 @@
         field_rsem,
         edge_ssem,
         edge_rsem,
+        shift_send,
+        shift_recv,
+        lists_recv,
+        lam_in,
+        omega_new,
+        packed_hi,
+        packed_lo,
+        shift_ssem,
+        shift_rsem,
+        lists_ssem,
+        lists_rsem,
     ) = refs[2 * count + 1 :]
     cas_hi, cas_lo, slope_hi, slope_lo, sine, dsine, inverse, bend, dbend, coef = table_vmem
     slab = lax.axis_index("slab")
@@ -176,96 +188,168 @@
         sent.append(copy)
         return copy
 
+    per_row = depth // BL
+    blocks = per_row * rows
+    sides = ((0, planes - 1), (1, 0))
+
+    def spread(row):
+        block_id = lax.broadcasted_iota(jnp.int32, (blocks, capacity), 0)
+        return jnp.where(block_id == row, 1.0, 0.0).astype(bf16)
+
     def make_code(s):
-        row_id = lax.broadcasted_iota(jnp.int32, (rows, capacity), 0)
-        block_id = lax.broadcasted_iota(jnp.int32, (depth, capacity), 0) >> (BL.bit_length() - 1)
-        for direction, x in ((0, planes - 1), (1, 0)):
-            at = (s * 2 + direction) * 2
-            row_hit = jnp.where(row_id == lists[at : at + 1, :], 1.0, 0.0).astype(bf16)
-            block_hit = jnp.where(block_id == lists[at + 1 : at + 2, :], 1.0, 0.0).astype(bf16)
-            hit = lax.dot_general(
-                row_hit, block_hit, (((1,), (1,)), ((), ())), preferred_element_type=f32
-            )
-            code[s, x] = shifts_in[s, x] + jnp.where(hit > 0.5, AWAY, 0)
-
-    def deposit(s, values, stay, leave):
+        ones = jnp.ones((capacity, BL), bf16)
+        for d, x in sides:
+            hit = dot(spread(lists[s * 2 + d : s * 2 + d + 1, :]), ones)
+            for b in range(per_row):
+                lanes = slice(b * BL, (b + 1) * BL)
+                away = jnp.where(hit[b * rows : (b + 1) * rows] > 0.5, AWAY, 0)
+                code[s, x, :, lanes] = shifts_in[s, x, :, lanes] + away
+
+    def stacked(plane):
+        return jnp.concatenate([plane[:, b * BL : (b + 1) * BL] for b in range(per_row)], 0)
+
+    def chooser(s, d):
+        block_id = lax.broadcasted_iota(jnp.int32, (capacity, blocks), 1)
+        column = lists_t[:, s * 2 + d : s * 2 + d + 1]
+        return jnp.where(block_id == column, 1.0, 0.0).astype(bf16)
+
+    def pack(s, values, leave):
+        for d, x in sides:
+            choose = chooser(s, d)
+            for c in range(3):
+                high, low = split(stacked(values[c, x]))
+                leave[d, :, c * BL : (c + 1) * BL] = dot(choose, high) + dot(choose, low)
+
+    def pack_shift(s):
+        for d, x in sides:
+            moved = stacked(shifts_in[s, x]).astype(f32).astype(bf16)
+            shift_send[s, d] = dot(chooser(s, d), moved)
+
+    def unpack(s, arrived, target):
+        for d in range(2):
+
+            def tile(i, carry):
+                at = pl.ds(pl.multiple_of(i * TILE, TILE), TILE)
+                amounts = shift_recv[s, d, at, :]
+                lane = lax.broadcasted_iota(jnp.int32, (TILE, BL), 1)
+                carried = [arrived[s, d, at, c * BL : (c + 1) * BL] for c in range(3)]
+                inside = [jnp.where(amounts == 0.0, v, 0.0) for v in carried]
+                across = [jnp.zeros((TILE, BL), f32) for v in carried]
+                for amount in (-2, -1, 1, 2):
+                    here = pltpu.roll(amounts, amount % BL, 1) == float(amount)
+                    wraps = lane < amount if amount > 0 else lane >= BL + amount
+                    for c in range(3):
+                        moved = jnp.where(here, pltpu.roll(carried[c], amount % BL, 1), 0.0)
+                        inside[c] = inside[c] + jnp.where(wraps, 0.0, moved)
+                        across[c] = across[c] + jnp.where(wraps, moved, 0.0)
+                for c in range(3):
+                    for part, value in ((0, inside[c]), (1, across[c])):
+                        high, low = split(value)
+                        lanes = slice((2 * c + part) * BL, (2 * c + part + 1) * BL)
+                        packed_hi[at, lanes] = high
+                        packed_lo[at, lanes] = low
+                return carry
+
+            lax.fori_loop(0, capacity // TILE, tile, 0)
+            place = spread(lists_recv[d, s * 2 + d : s * 2 + d + 1, :])
+            lower = lax.broadcasted_iota(jnp.int32, (rows, BL), 1) < BL // 2
+            for c in range(3):
+                lanes = slice(2 * c * BL, 2 * (c + 1) * BL)
+                full = dot(place, packed_hi[:, lanes]) + dot(place, packed_lo[:, lanes])
+
+                def piece(b, part):
+                    b = b % per_row
+                    return full[b * rows : (b + 1) * rows, part * BL : (part + 1) * BL]
+
+                for b in range(per_row):
+                    target[d, c, :, b * BL : (b + 1) * BL] = piece(b, 0) + jnp.where(
+                        lower, piece(b - 1, 1), piece(b + 1, 1)
+                    )
+
+    def deposit(s, values, stay):
         def tile(i, carry):
             at = pl.ds(pl.multiple_of(i * 8, 8), 8)
             for x in range(planes):
-                direction = 0 if x == planes - 1 else 1
                 mine = code[s, x, at, :]
                 carried = [values[c, x, at, :] for c in range(3)]
                 kept = [jnp.where(mine == 0, v, 0.0) for v in carried]
-                gone = [jnp.where(mine == AWAY, v, 0.0) for v in carried]
                 for amount in (-2, -1, 1, 2):
                     turned = pltpu.roll(mine, amount % depth, 1)
                     here = turned == amount
-                    there = turned == amount + AWAY
                     for c in range(3):
                         moved = pltpu.roll(carried[c], amount % depth, 1)
                         kept[c] = kept[c] + jnp.where(here, moved, 0.0)
-                        gone[c] = gone[c] + jnp.where(there, moved, 0.0)
                 for c in range(3):
                     stay[c, x, at, :] = kept[c]
-                    leave[direction, c, at, :] = gone[c]
             return carry
 
         lax.fori_loop(0, rows // 8, tile, 0)
 
-    def send_lam(s):
-        copies = []
-        for c in range(3):
-            copies.append(
-                [
-                    send(
-                        lam_send.at[s, d, c],
-                        lam_recv.at[s, d, c],
-                        lam_ssem.at[s, d, c],
-                        lam_rsem.at[s, d, c],
-                        {"slab": (onward, back)[d]},
-                    )
-                    for d in range(2)
-                ]
-            )
-        return copies
-
-    def send_omega(s):
+    def send_sides(s, source, target, ssem, rsem):
         return [
             send(
-                omega_send.at[s, d],
-                omega_recv.at[s, d],
-                omega_ssem.at[s, d],
-                omega_rsem.at[s, d],
+                source.at[s, d],
+                target.at[s, d],
+                ssem.at[s, d],
+                rsem.at[s, d],
                 {"slab": (onward, back)[d]},
             )
             for d in range(2)
         ]
 
+    def send_lam(s):
+        return send_sides(s, lam_send, lam_recv, lam_ssem, lam_rsem)
+
+    def send_omega(s):
+        return send_sides(s, omega_send, omega_recv, omega_ssem, omega_rsem)
+
+    def send_shift(s):
+        return send_sides(s, shift_send, shift_recv, shift_ssem, shift_rsem)
+
+    pack(0, adjoint_in, lam_send.at[0])
+    pack_shift(0)
+    pl.semaphore_wait(barrier, 2 + groups - 1)
+    list_copies = [
+        send(
+            lists,
+            lists_recv.at[d],
+            lists_ssem.at[d],
+            lists_rsem.at[d],
+            {"slab": (onward, back)[d]},
+        )
+        for d in range(2)
+    ]
+    shift_copies = send_shift(0)
+    lam_copies = send_lam(0)
     make_code(0)
-    deposit(0, adjoint_in, lam, lam_send.at[0])
-    pl.semaphore_wait(barrier, 2 + groups - 1)
-    lam_copies = send_lam(0)
     omega_load.wait()
-    deposit(0, omega_in.at[0], vortex.at[0], omega_send.at[0])
+    pack(0, omega_in.at[0], omega_send.at[0])
     omega_copies = send_omega(0)
+    deposit(0, adjoint_in, lam)
+    deposit(0, omega_in.at[0], vortex.at[0])
     for load in loads:
         load.wait()
+    for copy in list_copies:
+        copy.wait_recv()
 
     first = (lax.broadcasted_iota(jnp.int32, (1, depth), 1) == 0).astype(f32)
     for s in range(steps):
         edges[s, 0] = jnp.zeros((3, 8, depth), f32)
+        for copy in shift_copies:
+            copy.wait_recv()
+        for copy in lam_copies:
+            copy.wait_recv()
+        unpack(s, lam_recv, lam_in)
         for c in range(3):
-            for copy in lam_copies[c]:
-                copy.wait_recv()
 
             def gather(i, carry):
                 at = pl.ds(pl.multiple_of(i * TILE, TILE), TILE)
                 for x in range(planes):
                     total = lam[c, x, at, :]
                     if x == 0:
-                        total = total + lam_recv[s, 0, c, at, :]
+                        total = total + lam_in[0, c, at, :]
                     if x == planes - 1:
-                        total = total + lam_recv[s, 1, c, at, :]
+                        total = total + lam_in[1, c, at, :]
                     lam[c, x, at, :] = total
                     high, low = split(total)
                     to = pl.ds(pl.multiple_of(x * rows + i * TILE, TILE), TILE)
@@ -360,10 +444,14 @@
         arriving = omega_copies
         if s + 1 < steps:
             make_code(s + 1)
-            deposit(s + 1, omega_in.at[s + 1], vortex.at[s + 1], omega_send.at[s + 1])
+            pack_shift(s + 1)
+            shift_copies = send_shift(s + 1)
+            pack(s + 1, omega_in.at[s + 1], omega_send.at[s + 1])
             omega_copies = send_omega(s + 1)
+            deposit(s + 1, omega_in.at[s + 1], vortex.at[s + 1])
         for copy in arriving:
             copy.wait_recv()
+        unpack(s, omega_recv, omega_new)
         for copy in field_copies:
             copy.wait_recv()
         result = current if s + 1 < steps else out
@@ -373,9 +461,9 @@
             for x in range(planes):
                 w = [vortex[s, c, x, at, :] for c in range(3)]
                 if x == 0:
-                    w = [w[c] + omega_recv[s, 0, c, at, :] for c in range(3)]
+                    w = [w[c] + omega_new[0, c, at, :] for c in range(3)]
                 if x == planes - 1:
-                    w = [w[c] + omega_recv[s, 1, c, at, :] for c in range(3)]
+                    w = [w[c] + omega_new[1, c, at, :] for c in range(3)]
                 g = [field[s, c, x, at, :] for c in range(3)]
                 crossed = (
                     w[1] * g[2] - w[2] * g[1],
@@ -399,8 +487,9 @@
 
         lax.fori_loop(0, rows // 8, update, 0)
         if s + 1 < steps:
-            deposit(s + 1, current, lam, lam_send.at[s + 1])
+            pack(s + 1, current, lam_send.at[s + 1])
             lam_copies = send_lam(s + 1)
+            deposit(s + 1, current, lam)
     for copy in sent:
         copy.wait_send()
 
@@ -414,8 +503,8 @@
     per_row = depth // BL
     chosen = move_blocks[:, 0, 0]
     alive = jnp.arange(capacity, dtype=jnp.int32) < move_count[:, 0, 0][..., None]
-    lists = jnp.stack([jnp.where(alive, chosen // per_row, -1), chosen % per_row], 2)
-    lists = lists.reshape(steps * 4, capacity)
+    lists = jnp.where(alive, chosen % per_row * rows + chosen // per_row, -1)
+    lists = lists.reshape(steps * 2, capacity)
 
     cas, slope, sine, dsine, inverse, bend, dbend, coef = tables(rows, groups, depth)
     ends = np.zeros((rows, 128), np.float32)
@@ -440,10 +529,10 @@
         vm((3, planes, rows, depth), f32),
         vm((3, planes, rows, depth), f32),
         vm((steps, 3, planes, rows, depth), f32),
-        vm((steps, 2, 3, rows, depth), f32),
-        vm((steps, 2, 3, rows, depth), f32),
-        vm((steps, 2, 3, rows, depth), f32),
-        vm((steps, 2, 3, rows, depth), f32),
+        vm((steps, 2, capacity, 3 * BL), f32),
+        vm((steps, 2, capacity, 3 * BL), f32),
+        vm((steps, 2, capacity, 3 * BL), f32),
+        vm((steps, 2, capacity, 3 * BL), f32),
         vm((steps, 3, planes, rows, depth), f32),
         vm((steps, 2, 3, rows, depth), f32),
         vm((steps, groups, 3, 8, depth), f32),
@@ -454,27 +543,38 @@
         vm((4, planes * rows, depth), bf16),
         dma((count,)),
         dma((1,)),
-        dma((steps, 2, 3)),
-        dma((steps, 2, 3)),
+        dma((steps, 2)),
+        dma((steps, 2)),
         dma((steps, 2)),
         dma((steps, 2)),
         dma((steps, 2, 3)),
         dma((steps, 2, 3)),
         dma((steps, groups - 1)),
         dma((steps, groups - 1)),
+        vm((steps, 2, capacity, BL), f32),
+        vm((steps, 2, capacity, BL), f32),
+        vm((2, steps * 2, capacity), jnp.int32),
+        vm((2, 3, rows, depth), f32),
+        vm((2, 3, rows, depth), f32),
+        vm((capacity, 6 * BL), bf16),
+        vm((capacity, 6 * BL), bf16),
+        dma((steps, 2)),
+        dma((steps, 2)),
+        dma((2,)),
+        dma((2,)),
     ]
     sizes = (steps, planes, rows, depth, groups, slabs, capacity, count)
     local = pl.BlockSpec(memory_space=pltpu.VMEM)
     return pl.pallas_call(
         functools.partial(kernel, sizes),
         out_shape=jax.ShapeDtypeStruct(adjoint_vort.shape, f32),
-        in_specs=[local] * 4 + [pl.BlockSpec(memory_space=pl.ANY)] * (1 + count),
+        in_specs=[local] * 5 + [pl.BlockSpec(memory_space=pl.ANY)] * (1 + count),
         out_specs=local,
         scratch_shapes=scratch,
         compiler_params=pltpu.CompilerParams(
             collective_id=0, has_side_effects=True, vmem_limit_bytes=56 * 1024 * 1024
         ),
-    )(lists, adjoint_vort, cell_shift, jnp.asarray(ends), omega_ckpt, *held)
+    )(lists, lists.T, adjoint_vort, cell_shift, jnp.asarray(ends), omega_ckpt, *held)
 
 
 def solution(mesh):

time: 129 us -> 118 us (0.915)
  Pallas kernels: 124 us -> 110 us
  other arithmetic: 0.77 us -> 2.27 us
  local copies, waits for them, and re-layouts: 3.38 us -> 4.86 us
    pallas_call x1, Pallas kernels: 124 us -> 110 us  [shards(): pl.pallas_call(functools.partial(kernel, sizes), out_shape=jax.ShapeDtype...]
    unnamed x0 -> x1, other arithmetic: none -> 1.34 us
    unnamed x1 -> x2, local copies, waits for them, and re-layouts: 2.76 us -> 3.27 us
where the time goes in v1:
time: 118 us; the launch traced here: 117 us
  Pallas kernels  110 us (93%)
  local copies, waits for them, and re-layouts  4.86 us (4%)
  other arithmetic  2.27 us (2%)
    pallas_call x1, Pallas kernels, shards(): pl.pallas_call(functools.partial(kernel, sizes), out_shape=jax.ShapeDtype...  110 us
    unnamed x2, local copies, waits for them, and re-layouts  3.27 us

profile of v1, /device:TPU:0, one launch (start us, length us, event | category | flops | bytes accessed | tf_op | source)
XLA Modules:
  0.0 117.3 jit_solution(14079397515257170888)
XLA Ops:
  0.0 0.5 broadcast.31
  0.5 1.3 %reduce.3 = s32[2,2]{1,0:T(2,128)S(1)} reduce(s32[2,1,1,2]{3,2,1,0:T(1,128)} %param.19, s32[]{:T(128)} %broadcast.31), dimensions={1,2}, to_apply=%param.19.reduce_sub_computation.3 | reduce | bytes 36 | tf_op args[3]
  1.9 0.1 lt.23
  1.9 0.7 squeeze.3
  2.6 0.1 copy.19
  2.8 0.8 fusion.7.lists_t
  3.6 0.1 fusion.2
  3.7 0.7 copy.23.lists
  4.4 110.2 %shard_map.154 = f32[3,2,128,512]{3,2,1,0:T(8,128)} custom-call(s32[4,256]{1,0:T(4,128)} %copy.23.lists, s32[256,4]{1,0:T(8,128)} %fusion.7.lists_t, f32[3,2,128,512]{3,2,1,0:T(8,128)} %adjoint_in.1, s32[2,2,128,512]{3,2,1,0:T(8,128)} %shifts_in.1, f32[128,128]{1,0:T(8,128)} %constant.63.clone.ends, f32[2,3,2,128,512]{4,3,2,1,0:T(8,128)} %omega_hbm.1, ...), custom_call_target="tpu_custom_call" | custom-call | tf_op jit(solution)/shard_map/pallas_call | solution.py:568
  114.6 2.8 %copy.25 = f32[3,2,128,512]{3,2,1,0:T(8,128)} copy(f32[3,2,128,512]{3,2,1,0:T(8,128)} %shard_map.154) | data formatting | bytes 3145728
